TPU v7x, 512 devices: a whole 4x8x8 slice. The times are simulated.
512 devices in a mesh: lat: 16 (over x, y_hi, core), lon: 32 (over y_lo, z).
Axes of the slice: x: 4, y: 8 (y_hi: 2, y_lo: 4; y = y_hi * 4 + y_lo), z: 8, core: 2. Of those that a mesh axis runs over, the one named last changes fastest.
Arguments:
- tokens: bfloat16 [256, 512, 512], P('lat', 'lon'), may hold values from -6 to 6
- w_qkv0: bfloat16 [8, 192, 512], replicated, may hold values from -4 to 4
- w_out0: bfloat16 [512, 512], replicated, may hold values from -0.25 to 0.25
- gain0: float32 [512], replicated, may hold values from 0.25 to 1.75
- bias0: float32 [8, 225], replicated, may hold values from -4 to 4
- rel0: int32 [64, 64], replicated, may hold values from 0 to 224
- shift: int32 [2], replicated, may hold values from 1 to 7
- gain_merge: float32 [2048], replicated, may hold values from 0.25 to 1.75
- w_merge: bfloat16 [2048, 1024], P('lat'), may hold values from -0.125 to 0.125
- gain1: float32 [1024], replicated, may hold values from 0.25 to 1.75
- w_qkv1: bfloat16 [16, 192, 1024], P('lat'), may hold values from -4 to 4
- w_out1: bfloat16 [1024, 1024], P('lat'), may hold values from -0.1875 to 0.1875
- bias1: float32 [16, 225], P('lat'), may hold values from -4 to 4
- rel1: int32 [64, 64], replicated, may hold values from 0 to 224
Outputs:
- coarse_out: bfloat16 [128, 256, 1024], P('lat', 'lon')
All inputs are finite; a program needn't handle non-finite values.
Results may differ from a plain program's by a relative error of at most 0.03.
Values may be sent and summed in bfloat16 or wider, within the bound.
A program may use at most 64 MiB of HBM per device.

v0:
```python
import jax
import jax.numpy as jnp
from jax import lax
from jax.sharding import PartitionSpec as P

WIN = 8


EPS = 1e-05
NEG = -1e30


def with_halo(cells, sides, width):
    for axis, dim in sides:
        count = lax.axis_size(axis)
        head = lax.slice_in_dim(cells, 0, width, axis=dim)
        tail = lax.slice_in_dim(cells, cells.shape[dim] - width, cells.shape[dim], axis=dim)
        cells = jnp.concatenate(
            [
                lax.ppermute(tail, axis, [(i, (i + 1) % count) for i in range(count)]),
                cells,
                lax.ppermute(head, axis, [((i + 1) % count, i) for i in range(count)]),
            ],
            axis=dim,
        )
    return cells


def layer_norm(values, gain):
    mean = jnp.mean(values, axis=-1, keepdims=True)
    centred = values - mean
    spread = jnp.mean(centred * centred, axis=-1, keepdims=True)
    return centred * lax.rsqrt(spread + EPS) * gain


def bias_lookup(table, index):
    options = table.shape[1]
    onehot = (index[:, :, None] == jnp.arange(options, dtype=jnp.int32)[None, None, :]).astype(
        jnp.float32
    )
    return jnp.einsum("ijr,hr->hij", onehot, table, precision=lax.Precision.HIGHEST)


def times_rows(left, matrix):
    return lax.dot_general(
        left, matrix, (((1,), (1,)), ((), ())), preferred_element_type=jnp.float32
    )


def attend(qkv, bias, valid):
    head = qkv.shape[-1] // 3
    query = qkv[..., :head]
    keys = qkv[..., head : 2 * head]
    values = qkv[..., 2 * head :]
    scores = (
        jnp.einsum("wqhd,wkhd->whqk", query, keys, preferred_element_type=jnp.float32)
        * head ** (-0.5)
        + bias[None]
    )
    if valid is not None:
        scores = jnp.where(valid[:, None, None, :], scores, NEG)
    peak = jnp.max(scores, axis=-1, keepdims=True)
    weights = jnp.exp(scores - peak)
    probs = (weights / jnp.sum(weights, axis=-1, keepdims=True)).astype(jnp.bfloat16)
    mixed = jnp.einsum("whqk,wkhd->wqhd", probs, values, preferred_element_type=jnp.float32)
    return mixed.astype(jnp.bfloat16)


def on_device(
    tokens,
    w_qkv0,
    w_out0,
    gain0,
    bias0,
    rel0,
    shift,
    gain_merge,
    w_merge,
    gain1,
    w_qkv1,
    w_out1,
    bias1,
    rel1,
):
    rows, cols, chans = tokens.shape
    heads0 = w_qkv0.shape[0]
    head = w_qkv0.shape[1] // 3
    size = WIN * WIN
    lat_count = lax.axis_size("lat")
    lat_index = lax.axis_index("lat")
    zero = shift[0] * 0
    matrix0 = w_qkv0.reshape(-1, chans)
    padded = with_halo(tokens, (("lat", 0), ("lon", 1)), WIN - 1)
    span_r = rows + WIN
    span_c = cols + WIN
    region = lax.dynamic_slice(
        padded, (shift[0] - 1, shift[1] - 1, zero), (span_r, span_c, padded.shape[2])
    )
    normed = layer_norm(region.astype(jnp.float32), gain0).astype(jnp.bfloat16)
    qkv = times_rows(normed.reshape(-1, chans), matrix0)
    qkv = qkv.astype(jnp.bfloat16).reshape(region.shape[:2] + (heads0 * 3 * head,))
    down_n, across_n = (span_r // WIN, span_c // WIN)
    windows = (
        qkv.reshape(down_n, WIN, across_n, WIN, heads0, 3 * head)
        .transpose(0, 2, 1, 3, 4, 5)
        .reshape(down_n * across_n, size, heads0, 3 * head)
    )
    global_row = lat_index * rows + shift[0] - WIN + jnp.arange(span_r, dtype=jnp.int32)
    inside = (global_row >= 0) & (global_row < rows * lat_count)
    valid = jnp.broadcast_to(
        inside.reshape(down_n, 1, WIN, 1), (down_n, across_n, WIN, WIN)
    ).reshape(down_n * across_n, size)
    mixed = attend(windows, bias_lookup(bias0, rel0), valid)
    mixed = (
        mixed.reshape(down_n, across_n, WIN, WIN, chans)
        .transpose(0, 2, 1, 3, 4)
        .reshape(span_r, span_c, chans)
    )
    own = lax.dynamic_slice(mixed, (WIN - shift[0], WIN - shift[1], zero), (rows, cols, chans))
    projected = jnp.dot(own.reshape(-1, chans), w_out0, preferred_element_type=jnp.float32).reshape(
        rows, cols, chans
    )
    fine = (tokens.astype(jnp.float32) + projected).astype(jnp.bfloat16)
    half_r, half_c = (rows // 2, cols // 2)
    few = half_r * half_c
    blocks = (
        fine.reshape(half_r, 2, half_c, 2, chans).transpose(0, 2, 1, 3, 4).reshape(few, 4 * chans)
    )
    merged = layer_norm(blocks.astype(jnp.float32), gain_merge).astype(jnp.bfloat16)
    shares = lax.all_to_all(merged, "lat", split_axis=1, concat_axis=0, tiled=True)
    coarse_width = w_merge.shape[1]
    packed = w_qkv1.reshape(-1, coarse_width)
    coarse = lax.psum_scatter(
        jnp.dot(shares, w_merge, preferred_element_type=jnp.float32).astype(jnp.bfloat16),
        "lat",
        scatter_dimension=0,
        tiled=True,
    )
    normed1 = layer_norm(coarse.astype(jnp.float32), gain1).astype(jnp.bfloat16)
    qkv1 = times_rows(lax.all_gather(normed1, "lat", axis=0, tiled=True), packed).astype(
        jnp.bfloat16
    )
    local_heads = w_qkv1.shape[0]
    down_w, across_w = (half_r // WIN, half_c // WIN)
    windows1 = (
        qkv1.reshape(lat_count, down_w, WIN, across_w, WIN, local_heads, 3 * head)
        .transpose(0, 1, 3, 2, 4, 5, 6)
        .reshape(-1, size, local_heads, 3 * head)
    )
    mixed1 = attend(windows1, bias_lookup(bias1, rel1), None)
    attn1 = (
        mixed1.reshape(lat_count, down_w, across_w, WIN, WIN, local_heads * head)
        .transpose(0, 1, 3, 2, 4, 5)
        .reshape(lat_count * few, local_heads * head)
    )
    update = lax.psum_scatter(
        jnp.dot(attn1, w_out1, preferred_element_type=jnp.float32).astype(jnp.bfloat16),
        "lat",
        scatter_dimension=0,
        tiled=True,
    ).astype(jnp.float32)
    result = (coarse.astype(jnp.float32) + update).astype(jnp.bfloat16)
    return result.reshape(half_r, half_c, coarse_width)


def solution(mesh):
    placed = (
        P("lat", "lon", None),
        P(),
        P(),
        P(),
        P(),
        P(),
        P(),
        P(),
        P("lat", None),
        P(),
        P("lat", None, None),
        P("lat", None),
        P("lat", None),
        P(),
    )
    return jax.shard_map(
        on_device, mesh=mesh, in_specs=placed, out_specs=P("lat", "lon", None), check_vma=False
    )
```

profile of v0, /device:TPU:1, one launch (start us, length us, event | category | flops | bytes accessed | tf_op | source)
XLA Modules:
  0.0 353.3 jit_solution(15715223470290808207)
XLA Ops:
  7.6 8.8 %collective-permute-start = (bf16[7,16,512]{2,1,0:T(8,128)(2,1)S(1)}, bf16[7,16,512]{2,1,0:T(8,128)(2,1)S(1)}, u32[]{:S(2)}, u32[]{:S(2)}) collective-permute-start(bf16[7,16,512]{2,1,0:T(8,128)(2,1)S(1)} %get-tuple-element.10), channel_id=1, source_target_pairs={{0,32},{32,64},{64,96},{96,128},{128,160},{160,192},{192,224},{224... | collective-permute-start | bytes 344072 | tf_op jit(solution)/shard_map/ppermute | solution.py:20
  16.5 1.9 collective-permute-start.1
  18.4 1.3 fusion.55
  24.1 2.4 collective-permute-done.1
  26.6 4.0 %collective-permute-start.2 = (bf16[30,7,512]{2,1,0:T(8,128)(2,1)S(1)}, bf16[30,7,512]{2,1,0:T(8,128)(2,1)S(1)}, u32[]{:S(2)}, u32[]{:S(2)}) collective-permute-start(bf16[30,7,512]{2,1,0:T(8,128)(2,1)S(1)} %get-tuple-element.7), channel_id=1, source_target_pairs={{0,1},{1,2},{2,3},{3,4},{4,5},{5,6},{6,7},{7,8},{8,9},{9,10},{10,1... | collective-permute-start | bytes 645128 | tf_op jit(solution)/shard_map/ppermute | solution.py:20
  30.6 9.0 %collective-permute-start.3 = (bf16[30,7,512]{2,1,0:T(8,128)(2,1)S(1)}, bf16[30,7,512]{2,1,0:T(8,128)(2,1)S(1)}, u32[]{:S(2)}, u32[]{:S(2)}) collective-permute-start(bf16[30,7,512]{2,1,0:T(8,128)(2,1)S(1)} %get-tuple-element.8), channel_id=1, source_target_pairs={{1,0},{2,1},{3,2},{4,3},{5,4},{6,5},{7,6},{8,7},{9,8},{10,9},{11,1... | collective-permute-start | bytes 645128 | tf_op jit(solution)/shard_map/ppermute | solution.py:22
  39.7 3.2 fusion.28
  47.6 1.1 convolution_convert_fusion
  48.8 3.0 reshape_reshape.3
  51.8 3.7 %copy.36 = bf16[3,3,8,8,8,192]{5,3,2,4,1,0:T(8,128)(2,1)} copy(bf16[3,3,8,8,8,192]{5,4,3,1,2,0:T(8,128)(2,1)} %bitcast.76) | data formatting | bytes 3538944 | tf_op jit(solution)/shard_map/transpose | solution.py:105
  55.5 4.3 %fusion.56 = (f32[9,8,64]{2,1,0:T(8,128)S(1)}, f32[9,8,64,64]{2,3,1,0:T(8,128)}) fusion(f32[8,64,64]{1,2,0:T(8,128)S(1)} %copy-done.3, pred[9,64]{1,0:T(8,128)(4,1)S(1)} %broadcast_in_dim.17, bf16[9,64,8,192]{3,1,2,0:T(8,128)(2,1)} %bitcast.78), kind=kOutput, calls=%fused_computation.93 | convolution fusion | flops 39223360 | bytes 3099200 | tf_op jit(solution)/shard_map/sub | solution.py:63
  59.8 3.6 %fusion.9 = bf16[9,64,8,64]{1,3,2,0:T(8,128)(2,1)} fusion(f32[9,8,64,64]{2,3,1,0:T(8,128)} %get-tuple-element.14, bf16[9,64,8,192]{3,1,2,0:T(8,128)(2,1)} %bitcast.79, f32[9,8,64]{2,1,0:T(8,128)S(1)} %get-tuple-element.13), kind=kOutput, calls=%fused_computation.20 | convolution fusion | flops 38633472 | bytes 4147200 | tf_op jit(solution)/shard_map/whqk,wkhd->wqhd/dot_general | solution.py:65
  63.5 2.0 copy.40
  66.2 1.4 fusion.14
  69.7 19.6 %all_to_all.16 = bf16[64,16,128]{2,0,1:T(8,128)(2,1)S(1)} all-to-all(bf16[64,16,128]{2,0,1:T(8,128)(2,1)S(1)} %copy.43), channel_id=1, replica_groups=mesh['lat'=16,'lon'=32] {'lat'}, dimensions={1} | all-to-all | bytes 524288 | tf_op jit(solution)/shard_map/all_to_all | solution.py:130
  89.2 2.0 convolution_convert_fusion.2
  91.4 88.0 %reduce-scatter.3.cloned.1.call-done = bf16[64,1024]{1,0:T(8,128)(2,1)} async-done(((bf16[1024,1024]{1,0:T(8,128)(2,1)}), bf16[64,1024]{1,0:T(8,128)(2,1)}) %reduce-scatter.3.cloned.1.call-update) | async-done | bytes 131088 | tf_op jit(solution)/shard_map/reduce_scatter | solution.py:133
  181.6 1.7 fusion.37
  183.5 2.8 fusion.3
  186.4 61.5 %all-gather.2.cloned.1.call-done = bf16[1024,1024]{1,0:T(8,128)(2,1)} async-done(((bf16[64,1024]{1,0:T(8,128)(2,1)}), bf16[1024,1024]{1,0:T(8,128)(2,1)}) %all-gather.2.cloned.1.call-update) | async-done | bytes 2097168 | tf_op jit(solution)/shard_map/all_gather | solution.py:140
  248.0 2.4 convolution_convert_fusion.4
  251.8 2.1 convolution_convert_fusion.1
  253.9 91.2 %reduce-scatter.5.cloned.1.call-done = bf16[64,1024]{1,0:T(8,128)(2,1)} async-done(((bf16[1024,1024]{1,0:T(8,128)(2,1)}), bf16[64,1024]{1,0:T(8,128)(2,1)}) %reduce-scatter.5.cloned.1.call-update) | async-done | bytes 131088 | tf_op jit(solution)/shard_map/reduce_scatter | solution.py:156
  345.2 1.6 fusion.41
  (73 shorter events, 11.1 us)
Async XLA Ops:
  6.5 41.1 %copy-start = (bf16[8,192,512]{2,1,0:T(8,128)(2,1)S(1)}, bf16[8,192,512]{2,1,0:T(8,128)(2,1)}, u32[]{:S(2)}) copy-start(bf16[8,192,512]{2,1,0:T(8,128)(2,1)} %param.15) | copy-start | bytes 4718596
  6.5 33.1 %copy-start.11 = (f32[8,225]{1,0:T(8,128)S(1)}, f32[8,225]{1,0:T(8,128)}, u32[]{:S(2)}) copy-start(f32[8,225]{1,0:T(8,128)} %param.18) | copy-start | bytes 21604
  6.5 33.1 %copy-start.9 = (s32[64,64]{1,0:T(8,128)S(1)}, s32[64,64]{1,0:T(8,128)}, u32[]{:S(2)}) copy-start(s32[64,64]{1,0:T(8,128)} %param.19) | copy-start | bytes 49156
  6.5 172.8 %reduce-scatter.3.cloned.1.call-start = ((), (), s32[]{:S(2)}) async-start(), calls=%async_computation.3 | async-start | bytes 2228224 | tf_op jit(solution)/shard_map/reduce_scatter | solution.py:133
  7.6 15.5 %collective-permute-start = (bf16[7,16,512]{2,1,0:T(8,128)(2,1)S(1)}, bf16[7,16,512]{2,1,0:T(8,128)(2,1)S(1)}, u32[]{:S(2)}, u32[]{:S(2)}) collective-permute-start(bf16[7,16,512]{2,1,0:T(8,128)(2,1)S(1)} %get-tuple-element.10), channel_id=1, source_target_pairs={{0,32},{32,64},{64,96},{96,128},{128,160},{160,192},{192,224},{224... | collective-permute-start | bytes 344072 | tf_op jit(solution)/shard_map/ppermute | solution.py:20
  16.5 10.0 %collective-permute-start.1 = (bf16[7,16,512]{2,1,0:T(8,128)(2,1)S(1)}, bf16[7,16,512]{2,1,0:T(8,128)(2,1)S(1)}, u32[]{:S(2)}, u32[]{:S(2)}) collective-permute-start(bf16[7,16,512]{2,1,0:T(8,128)(2,1)S(1)} %get-tuple-element.9), channel_id=1, source_target_pairs={{32,0},{64,32},{96,64},{128,96},{160,128},{192,160},{224,192},{256... | collective-permute-start | bytes 344072 | tf_op jit(solution)/shard_map/ppermute | solution.py:22
  26.6 20.8 %copy-start.7 = (f32[512]{0:T(512)S(1)}, f32[512]{0:T(512)}, u32[]{:S(2)}) copy-start(f32[512]{0:T(512)} %param.17) | copy-start | bytes 6148
  26.6 19.7 %collective-permute-start.2 = (bf16[30,7,512]{2,1,0:T(8,128)(2,1)S(1)}, bf16[30,7,512]{2,1,0:T(8,128)(2,1)S(1)}, u32[]{:S(2)}, u32[]{:S(2)}) collective-permute-start(bf16[30,7,512]{2,1,0:T(8,128)(2,1)S(1)} %get-tuple-element.7), channel_id=1, source_target_pairs={{0,1},{1,2},{2,3},{3,4},{4,5},{5,6},{6,7},{7,8},{8,9},{9,10},{10,1... | collective-permute-start | bytes 645128 | tf_op jit(solution)/shard_map/ppermute | solution.py:20
  30.6 15.7 %collective-permute-start.3 = (bf16[30,7,512]{2,1,0:T(8,128)(2,1)S(1)}, bf16[30,7,512]{2,1,0:T(8,128)(2,1)S(1)}, u32[]{:S(2)}, u32[]{:S(2)}) collective-permute-start(bf16[30,7,512]{2,1,0:T(8,128)(2,1)S(1)} %get-tuple-element.8), channel_id=1, source_target_pairs={{1,0},{2,1},{3,2},{4,3},{5,4},{6,5},{7,6},{8,7},{9,8},{10,9},{11,1... | collective-permute-start | bytes 645128 | tf_op jit(solution)/shard_map/ppermute | solution.py:22
  51.8 3.7 %copy-start.3 = (f32[8,64,64]{1,2,0:T(8,128)S(1)}, f32[8,64,64]{1,2,0:T(8,128)}, u32[]{:S(2)}) copy-start(f32[8,64,64]{1,2,0:T(8,128)} %copy.37) | copy-start | bytes 393220
  67.7 1.7 copy-start.5
  68.2 21.0 %copy-start.2 = (bf16[128,1024]{1,0:T(8,128)(2,1)S(1)}, bf16[128,1024]{1,0:T(8,128)(2,1)}, u32[]{:S(2)}) copy-start(bf16[128,1024]{1,0:T(8,128)(2,1)} %param.22) | copy-start | bytes 786436
  89.2 92.3 %copy-start.6 = (f32[1024]{0:T(1024)S(1)}, f32[1024]{0:T(1024)}, u32[]{:S(2)}) copy-start(f32[1024]{0:T(1024)} %param.23) | copy-start | bytes 12292
  89.2 94.2 %copy-start.10 = (s32[64,64]{1,0:T(8,128)S(1)}, s32[64,64]{1,0:T(8,128)}, u32[]{:S(2)}) copy-start(s32[64,64]{1,0:T(8,128)} %param.27) | copy-start | bytes 49156
  89.2 94.3 %copy-start.12 = (f32[1,225]{1,0:T(1,128)S(1)}, f32[1,225]{1,0:T(1,128)}, u32[]{:S(2)}) copy-start(f32[1,225]{1,0:T(1,128)} %param.26) | copy-start | bytes 2704
  91.3 156.7 %copy-start.8 = (bf16[1,192,1024]{2,1,0:T(8,128)(2,1)S(1)}, bf16[1,192,1024]{2,1,0:T(8,128)(2,1)}, u32[]{:S(2)}) copy-start(bf16[1,192,1024]{2,1,0:T(8,128)(2,1)} %param.24) | copy-start | bytes 1179652
  91.3 156.6 %all-gather.2.cloned.1.call-start = ((), (), s32[]{:S(2)}) async-start(), calls=%async_computation.4 | async-start | bytes 2228224 | tf_op jit(solution)/shard_map/all_gather | solution.py:140
  183.2 161.9 %reduce-scatter.5.cloned.1.call-start = ((), (), s32[]{:S(2)}) async-start(), calls=%async_computation.5 | async-start | bytes 2228224 | tf_op jit(solution)/shard_map/reduce_scatter | solution.py:156
  250.9 0.9 copy-start.4
  251.8 93.3 %copy-start.1 = (bf16[64,1024]{1,0:T(8,128)(2,1)S(1)}, bf16[64,1024]{1,0:T(8,128)(2,1)}, u32[]{:S(2)}) copy-start(bf16[64,1024]{1,0:T(8,128)(2,1)} %reduce-scatter.3.cloned.1.call-done) | copy-start | bytes 393220
Sparse Core Ops, SparseCore 0:
  91.4 87.8 reduce-scatter.2
  183.4 64.5 all-gather.1
  254.1 91.0 reduce-scatter.4
where the time goes:
time: 354 us; the launch traced here: 353 us
  waiting for transfers between devices  243 us (69%)
  starting transfers between devices  24.1 us (7%)
  matrix products  23.7 us (7%)
  blocking collectives  19.6 us (6%)
  between operations  19.3 us (5%)
  local copies, waits for them, and re-layouts  15.7 us (4%)
  other arithmetic  7.7 us (2%)
    reduce_scatter x1, waiting for transfers between devices, on_device(): lax.psum_scatter(jnp.dot(attn1, w_out1, preferred_element_type=jnp.float3...  91.2 us
    reduce_scatter x1, waiting for transfers between devices, on_device(): lax.psum_scatter(jnp.dot(shares, w_merge, preferred_element_type=jnp.floa...  88 us
    all_gather x1, waiting for transfers between devices, on_device(): lax.all_gather(normed1, 'lat', axis=0, tiled=True)  61.5 us
    all_to_all x1, blocking collectives, on_device(): lax.all_to_all(merged, 'lat', split_axis=1, concat_axis=0, tiled=True)  19.6 us
    ppermute x2, starting transfers between devices, with_halo(): lax.ppermute(tail, axis, [(i, (i + 1) % count) for i in range(count)])  12.8 us
    ppermute x2, starting transfers between devices, with_halo(): lax.ppermute(head, axis, [((i + 1) % count, i) for i in range(count)])  11 us
  transfers between devices with their start and end apart: 7, of which 4 were waited for; matrix products, arithmetic and copies ran while one was open for 3% of the time, Pallas kernels for 0%

commit v1 on v0

v1 whole, which is shorter than its diff:
```python
import functools

import jax
import jax.numpy as jnp
from jax import lax
from jax.experimental import pallas as pl
from jax.experimental.pallas import tpu as pltpu
from jax.sharding import PartitionSpec as P

WIN = 8
EPS = 1e-05
NEG = -1e30
MESH = pl.DeviceIdType.MESH
F32 = jnp.float32
BF16 = jnp.bfloat16
PAIR_ORDER = (0, 2, 4, 6, 1, 3, 5, 7)


def place():
    lat = lax.axis_index("lat")
    lon = lax.axis_index("lon")
    x = lax.div(lat, 4)
    half = lax.rem(lax.div(lat, 2), 2)
    core = lax.rem(lat, 2)
    y = half * 4 + lax.div(lon, 8)
    z = lax.rem(lon, 8)
    return lat, lon, x, y, z, core


def at(x, y, z, core):
    return (
        lax.rem(x + 4, 4) * 4 + lax.div(y, 4) * 2 + core,
        lax.rem(y, 4) * 8 + lax.rem(z + 8, 8),
    )


def dot_nt(left, right):
    return lax.dot_general(left, right, (((1,), (1,)), ((), ())), preferred_element_type=F32)


def dot_nn(left, right):
    return jnp.dot(left, right, preferred_element_type=F32)


def norm_rows(values, gain):
    mean = jnp.mean(values, axis=-1, keepdims=True)
    centred = values - mean
    spread = jnp.mean(centred * centred, axis=-1, keepdims=True)
    return centred * lax.rsqrt(spread + EPS) * gain


def lane_masks():
    lane = lax.broadcasted_iota(jnp.int32, (64, 128), 1)
    return lane < 64


def attend_pair(q2, k2, v2, bias, mask):
    low = lane_masks()
    low_b = low.astype(F32).astype(BF16)
    high_b = (1.0 - low.astype(F32)).astype(BF16)
    keys = jnp.concatenate([k2 * low_b, k2 * high_b], axis=0)
    scores = dot_nt(q2, keys) + bias
    if mask is not None:
        scores = scores + mask
    peak_a = jnp.max(jnp.where(low, scores, -jnp.inf), axis=-1, keepdims=True)
    peak_b = jnp.max(jnp.where(low, -jnp.inf, scores), axis=-1, keepdims=True)
    weights = jnp.exp(scores - jnp.where(low, peak_a, peak_b)).astype(BF16)
    values = jnp.concatenate([v2 * low_b, v2 * high_b], axis=0)
    ones = jnp.concatenate([low_b, high_b], axis=0)
    mixed = dot_nn(weights, jnp.concatenate([values, ones], axis=1))
    return (mixed[:, :128] / mixed[:, 128:]).astype(BF16)


def fill_bias(table, rel2, out):
    coarse_part = table.astype(BF16).astype(F32)
    split = jnp.concatenate([coarse_part, table - coarse_part], axis=0).astype(BF16)
    entry = lax.broadcasted_iota(jnp.int32, (256, 128), 0)
    low = lax.broadcasted_iota(jnp.int32, (4, 128), 1) < 64

    def step(p, carry):
        row = rel2[pl.ds(p, 1), :]
        onehot = jnp.where(entry == row, 1.0, 0.0).astype(BF16)
        both = dot_nn(split, onehot)
        both = both[:8] + both[8:]
        packed = jnp.where(low, both[:4], both[4:])
        for t in range(4):
            out[t, pl.ds(p, 1), :] = packed[t : t + 1]
        return carry

    lax.fori_loop(0, 64, step, 0, unroll=4)


def kernel(
    shift, tok, w0, wo0, g0, rel0, tab0, gm, wm, g1, wq, wo, tab1, rel1,
    out,
    fine_ref, hq, wide_m, wide_q, wide_o, tabs, b0, b1, mg, mo,
    part_s, part_r, both, upd_s, upd_r, coarse_ref, attn, ss, rs, ls,
):
    lat, lon, x, y, z, core = place()
    half = lax.div(y, 4)
    a = shift[0]
    b = shift[1]

    here = (x, y, z, core)
    to_xp, to_xm, to_x2 = at(x + 1, y, z, core), at(x - 1, y, z, core), at(x + 2, y, z, core)
    to_mir = at(x, 7 - y, z, core)
    to_zp, to_zm = at(x, y, z + 1, core), at(x, y, z - 1, core)
    to_core = at(x, y, z, 1 - core)
    up, down = lax.rem(lat + 15, 16), lax.rem(lat + 1, 16)
    left, right = lax.rem(lon + 31, 32), lax.rem(lon + 1, 32)

    barrier = pltpu.get_barrier_semaphore()
    partners = [
        to_xp, to_xm, to_x2, to_mir, to_zp, to_zm, to_core,
        (up, lon), (down, lon), (lat, left), (lat, right),
        (up, left), (up, right), (down, left), (down, right),
    ]
    for dev in partners:
        pl.semaphore_signal(barrier, inc=1, device_id=dev, device_id_type=MESH)
    pl.semaphore_wait(barrier, len(partners))

    made = []

    def remote(src, dst, dev):
        k = len(made)
        copy = pltpu.make_async_remote_copy(
            src_ref=src, dst_ref=dst, send_sem=ss.at[k], recv_sem=rs.at[k],
            device_id=dev, device_id_type=MESH,
        )
        made.append(copy)
        return copy

    halo_lon = [
        remote(tok.at[1], hq.at[4], (lat, right)),
        remote(tok.at[3], hq.at[8], (lat, right)),
        remote(tok.at[0], hq.at[7], (lat, left)),
        remote(tok.at[2], hq.at[11], (lat, left)),
    ]
    halo_lat = [
        remote(tok.at[pl.ds(2, 2)], hq.at[pl.ds(1, 2)], (down, lon)),
        remote(tok.at[pl.ds(0, 2)], hq.at[pl.ds(13, 2)], (up, lon)),
        remote(tok.at[3], hq.at[0], (down, right)),
        remote(tok.at[2], hq.at[3], (down, left)),
        remote(tok.at[1], hq.at[12], (up, right)),
        remote(tok.at[0], hq.at[15], (up, left)),
    ]
    for copy in halo_lat + halo_lon:
        copy.start()

    parity = lax.rem(z, 2)
    pieces = [(wm, wide_m, 128), (wq, wide_q, 192), (wo, wide_o, 64)]
    first, second, share_a, share_b, locals_ = [], [], [], [], []
    tab_first = [
        remote(tab1, tabs.at[2], to_xp),
        remote(tab1, tabs.at[1], to_xm),
        remote(tab1, tabs.at[3], to_x2),
        remote(tab1, tabs.at[4], to_mir),
    ]
    tab_second = [
        remote(tabs.at[4], tabs.at[6], to_xp),
        remote(tabs.at[4], tabs.at[5], to_xm),
        remote(tabs.at[4], tabs.at[7], to_x2),
    ]
    for n, (src, wide, rows) in enumerate(pieces):
        size = rows // 2
        start = pl.multiple_of(parity * size, 16)
        mine = pl.ds(start, size)
        quarter_a = pl.ds(start, size // 2)
        quarter_b = pl.ds(pl.multiple_of(start + size // 2, 16), size // 2)
        first.append([
            remote(src.at[mine], wide.at[2, mine], to_xp),
            remote(src.at[mine], wide.at[1, mine], to_xm),
            remote(src.at[mine], wide.at[3, mine], to_x2),
            remote(src.at[mine], wide.at[4, mine], to_mir),
        ])
        far = (
            remote(wide.at[4, mine], wide.at[7, mine], to_x2)
            if n == 1
            else remote(wide.at[3, mine], wide.at[7, mine], to_mir)
        )
        second.append([
            remote(wide.at[4, mine], wide.at[6, mine], to_xp),
            remote(wide.at[4, mine], wide.at[5, mine], to_xm),
            far,
        ])
        share_a.append([
            remote(wide.at[pl.ds(1, 4), quarter_a], wide.at[pl.ds(1, 4), quarter_a], to_zp),
            remote(wide.at[pl.ds(1, 4), quarter_b], wide.at[pl.ds(1, 4), quarter_b], to_zm),
        ])
        share_b.append([
            remote(wide.at[pl.ds(5, 3), quarter_a], wide.at[pl.ds(5, 3), quarter_a], to_zp),
            remote(wide.at[pl.ds(5, 3), quarter_b], wide.at[pl.ds(5, 3), quarter_b], to_zm),
        ])
        locals_.append(pltpu.make_async_copy(src, wide.at[0], ls.at[n]))
    locals_.append(pltpu.make_async_copy(tab1, tabs.at[0], ls.at[3]))

    def start_all(copies):
        for copy in copies:
            copy.start()

    def recv_all(copies):
        for copy in copies:
            copy.wait_recv()

    start_all(tab_first)
    for n in range(3):
        start_all(first[n])
    start_all(locals_)

    def stage_two(n):
        recv_all(first[n])
        start_all(second[n])
        start_all(share_a[n])

    def stage_three(n):
        recv_all(second[n])
        start_all(share_b[n])

    for i in range(2):
        for j in range(2):
            hq[4 * i + j + 5] = tok[2 * i + j]
    want = lax.broadcasted_iota(jnp.int32, (192, 1), 0)
    want_r = a + ((want & 63) >> 3)
    want_c = b + 8 * (want >> 6) + (want & 7)
    want = (want_r >> 3) * 256 + (want_c >> 3) * 64 + (want_r & 7) * 8 + (want_c & 7)
    pick = lax.broadcasted_iota(jnp.int32, (192, 512), 1) == want
    pick = jnp.where(pick, 1.0, 0.0).astype(BF16)
    fill_bias(tab0[...], rel0, b0)

    def window_row(k, carry):
        i = lax.rem(k + 1, 3)

        @pl.when(k == 0)
        def _():
            recv_all(halo_lon)

        @pl.when(k == 1)
        def _():
            stage_two(0)
            recv_all(halo_lat)

        @pl.when(k == 2)
        def _():
            stage_two(1)
            stage_three(0)

        cells = dot_nn(pick, hq[pl.ds(4 * i, 8)].reshape(512, 512))
        normed = norm_rows(cells, g0[...]).astype(BF16)
        query = (dot_nt(normed, w0[:, 0:64, :].reshape(512, 512)) * 0.125).astype(BF16)
        keys = dot_nt(normed, w0[:, 64:128, :].reshape(512, 512)).astype(BF16)
        values = dot_nt(normed, w0[:, 128:192, :].reshape(512, 512)).astype(BF16)
        lane = lax.broadcasted_iota(jnp.int32, (1, 128), 1)
        row = lat * 16 + a - 8 + 8 * i + ((lane & 63) >> 3)
        mask = jnp.where((row >= 0) & (row < 256), 0.0, NEG)
        for w in range(3):
            rows = slice(64 * w, 64 * w + 64)
            for t in range(4):
                cols = slice(128 * t, 128 * t + 128)
                attn[rows, cols] = attend_pair(
                    query[rows, cols], keys[rows, cols], values[rows, cols], b0[t], mask
                )
        fine = cells + dot_nn(attn[...], wo0[...])
        fine_ref[pl.ds(pl.multiple_of(192 * i, 64), 192), :] = fine.astype(BF16)
        return carry

    lax.fori_loop(0, 3, window_row, 0)
    stage_two(2)
    stage_three(1)
    recv_all(tab_first)
    start_all(tab_second)

    want = lax.broadcasted_iota(jnp.int32, (256, 1), 0)
    want_r = 8 - a + 2 * ((want >> 3) & 7) + (want >> 7)
    want_c = 8 - b + 2 * (want & 7) + ((want >> 6) & 1)
    want = (want_r >> 3) * 192 + (want_c >> 3) * 64 + (want_r & 7) * 8 + (want_c & 7)
    pick = lax.broadcasted_iota(jnp.int32, (256, 576), 1) == want
    pick = jnp.where(pick, 1.0, 0.0).astype(BF16)
    picked = dot_nn(pick, fine_ref[...])
    blocks = [picked[64 * k : 64 * k + 64] for k in range(4)]
    total = sum(jnp.sum(block, axis=-1, keepdims=True) for block in blocks)
    mean = total * (1.0 / 2048)
    blocks = [block - mean for block in blocks]
    spread = sum(jnp.sum(block * block, axis=-1, keepdims=True) for block in blocks)
    scale = lax.rsqrt(spread * (1.0 / 2048) + EPS)
    for k in range(4):
        merged = (blocks[k] * scale * gm[:, 512 * k : 512 * k + 512]).astype(BF16)
        for m in range(4):
            chunk = 4 * k + m
            mg[chunk % 2, chunk // 2] = merged[:, 128 * m : 128 * m + 128]

    give_merged = remote(mg.at[1 - core], mo, to_core)
    give_part = remote(part_s, part_r, to_core)
    give_norm = remote(both.at[0], both.at[1], to_core)
    give_upd = remote(upd_s, upd_r, to_core)
    give_merged.start()
    stage_three(2)
    recv_all(tab_second)
    for copy in locals_:
        copy.wait()
    sub = lax.broadcasted_iota(jnp.int32, (8, 256), 0)
    table = jnp.zeros((8, 256), F32)
    for n, slot in enumerate(PAIR_ORDER):
        table = jnp.where(sub == n, tabs[slot], table)
    fill_bias(table, rel1, b1)

    recv_all(share_a[0])
    recv_all(share_b[0])
    give_merged.wait_recv()
    slots = [
        2 * lax.rem(x + step, 4) + side for side in (half, 1 - half) for step in (0, 1, 3, 2)
    ]
    mine = jnp.concatenate([mg[core, slot] for slot in slots], axis=1)
    theirs = jnp.concatenate([mo[slot] for slot in slots], axis=1)
    merged = jnp.concatenate([theirs, mine], axis=0)
    partial = dot_nn(merged, wide_m[...].reshape(1024, 1024))
    part_s[...] = partial[:64].astype(BF16)
    give_part.start()
    give_part.wait_recv()
    coarse = (partial[64:] + part_r[...].astype(F32)).astype(BF16)
    coarse_ref[...] = coarse
    both[0] = norm_rows(coarse.astype(F32), g1[...]).astype(BF16)
    give_norm.start()
    recv_all(share_a[1])
    recv_all(share_b[1])
    give_norm.wait_recv()
    normed = both[...].reshape(128, 1024)
    query = (dot_nt(normed, wide_q[:, 0:64, :].reshape(512, 1024)) * 0.125).astype(BF16)
    keys = dot_nt(normed, wide_q[:, 64:128, :].reshape(512, 1024)).astype(BF16)
    values = dot_nt(normed, wide_q[:, 128:192, :].reshape(512, 1024)).astype(BF16)
    for w in range(2):
        rows = slice(64 * w, 64 * w + 64)
        for t in range(4):
            cols = slice(128 * t, 128 * t + 128)
            attn[rows, cols] = attend_pair(
                query[rows, cols], keys[rows, cols], values[rows, cols], b1[t], None
            )
    recv_all(share_a[2])
    recv_all(share_b[2])
    update = dot_nn(attn[0:128, :], wide_o[...].reshape(512, 1024))
    upd_s[...] = update[64:].astype(BF16)
    give_upd.start()
    give_upd.wait_recv()
    out[...] = (coarse_ref[...].astype(F32) + update[:64] + upd_r[...].astype(F32)).astype(BF16)
    for copy in made:
        copy.wait_send()


COPIES = 10 + 7 + 3 * 11 + 4


def on_device(
    tokens, w_qkv0, w_out0, gain0, bias0, rel0, shift, gain_merge, w_merge, gain1, w_qkv1,
    w_out1, bias1, rel1,
):
    tok = tokens.reshape(2, 8, 2, 8, 512).transpose(0, 2, 1, 3, 4).reshape(4, 64, 512)
    tab0 = jnp.pad(bias0, ((0, 0), (0, 31)))
    tab0 = jnp.concatenate([tab0[0::2], tab0[1::2]], axis=0)
    tab1 = jnp.broadcast_to(jnp.pad(bias1, ((0, 0), (0, 31))), (8, 256))
    twice0 = jnp.concatenate([rel0, rel0], axis=1)
    twice1 = jnp.concatenate([rel1, rel1], axis=1)
    vmem = pl.BlockSpec(memory_space=pltpu.VMEM)
    smem = pl.BlockSpec(memory_space=pltpu.SMEM)
    result = pl.pallas_call(
        kernel,
        out_shape=jax.ShapeDtypeStruct((64, 1024), BF16),
        in_specs=[smem] + [vmem] * 13,
        out_specs=vmem,
        scratch_shapes=[
            pltpu.VMEM((576, 512), BF16),
            pltpu.VMEM((16, 64, 512), BF16),
            pltpu.VMEM((8, 128, 1024), BF16),
            pltpu.VMEM((8, 192, 1024), BF16),
            pltpu.VMEM((8, 64, 1024), BF16),
            pltpu.VMEM((8, 8, 256), F32),
            pltpu.VMEM((4, 64, 128), F32),
            pltpu.VMEM((4, 64, 128), F32),
            pltpu.VMEM((2, 8, 64, 128), BF16),
            pltpu.VMEM((8, 64, 128), BF16),
            pltpu.VMEM((64, 1024), BF16),
            pltpu.VMEM((64, 1024), BF16),
            pltpu.VMEM((2, 64, 1024), BF16),
            pltpu.VMEM((64, 1024), BF16),
            pltpu.VMEM((64, 1024), BF16),
            pltpu.VMEM((64, 1024), BF16),
            pltpu.VMEM((192, 512), BF16),
            pltpu.SemaphoreType.DMA((COPIES,)),
            pltpu.SemaphoreType.DMA((COPIES,)),
            pltpu.SemaphoreType.DMA((4,)),
        ],
        compiler_params=pltpu.CompilerParams(
            collective_id=0, has_side_effects=True, vmem_limit_bytes=48 << 20
        ),
        name="swin",
    )(
        shift, tok, w_qkv0, w_out0, gain0.reshape(1, 512), twice0, tab0,
        gain_merge.reshape(1, 2048), w_merge, gain1.reshape(1, 1024),
        w_qkv1.reshape(192, 1024), w_out1, tab1, twice1,
    )
    return result.reshape(8, 8, 1024)


def solution(mesh):
    placed = (
        P("lat", "lon", None),
        P(),
        P(),
        P(),
        P(),
        P(),
        P(),
        P(),
        P("lat", None),
        P(),
        P("lat", None, None),
        P("lat", None),
        P("lat", None),
        P(),
    )
    return jax.shard_map(
        on_device, mesh=mesh, in_specs=placed, out_specs=P("lat", "lon", None), check_vma=False
    )
```

time: 354 us -> 90.8 us (0.26)
  the two profiles are of different devices: /device:TPU:1 before, /device:TPU:57 now
where the time goes in v1:
time: 90.8 us; the launch traced here: 90.3 us
  Pallas kernels  78.2 us (86%)
  local copies, waits for them, and re-layouts  11.1 us (12%)
  other arithmetic  0.93 us (1%)
    pallas_call x1, Pallas kernels, on_device(): pl.pallas_call(kernel, out_shape=jax.ShapeDtypeStruct((64, 1024), BF16),...  78.2 us
    unnamed x19, local copies, waits for them, and re-layouts  8.67 us

profile of v1, /device:TPU:57, one launch (start us, length us, event | category | flops | bytes accessed | tf_op | source)
XLA Modules:
  0.0 90.3 jit_solution(4372086034366016909)
XLA Ops:
  0.0 0.7 pad.9
  0.7 0.7 pad.8
  1.4 0.9 %pad_add_fusion = (s32[64,128]{1,0:T(8,128)S(1)}, s32[64,128]{1,0:T(8,128)S(1)}) fusion(s32[64,64]{1,0:T(8,128)} %param.19, s32[64,64]{1,0:T(8,128)} %param.27), kind=kLoop, calls=%fused_computation | loop fusion | flops 16384 | bytes 98304 | tf_op jit(solution)/shard_map/concatenate | solution.py:359
  2.4 1.0 %copy.15 = bf16[2,8,2,8,512]{4,3,1,2,0:T(8,128)(2,1)S(1)} copy(bf16[2,8,2,8,512]{4,3,2,1,0:T(8,128)(2,1)} %bitcast.16) | data formatting | bytes 524288 | tf_op jit(solution)/shard_map/reshape | solution.py:355
  3.3 0.0 copy-start
  3.4 1.4 %copy-done = bf16[8,192,512]{2,1,0:T(8,128)(2,1)S(1)} copy-done((bf16[8,192,512]{2,1,0:T(8,128)(2,1)S(1)}, bf16[8,192,512]{2,1,0:T(8,128)(2,1)}, u32[]{:S(2)}) %copy-start) | copy-done | bytes 1572888
  4.8 0.0 copy-start.1
  4.8 1.0 %copy-done.1 = bf16[512,512]{1,0:T(8,128)(2,1)S(1)} copy-done((bf16[512,512]{1,0:T(8,128)(2,1)S(1)}, bf16[512,512]{1,0:T(8,128)(2,1)}, u32[]{:S(2)}) %copy-start.1) | copy-done | bytes 524312
  5.8 0.0 copy-start.2
  5.8 1.0 %copy-done.2 = bf16[1,192,1024]{2,1,0:T(8,128)(2,1)S(1)} copy-done((bf16[1,192,1024]{2,1,0:T(8,128)(2,1)S(1)}, bf16[1,192,1024]{2,1,0:T(8,128)(2,1)}, u32[]{:S(2)}) %copy-start.2) | copy-done | bytes 393240
  6.8 0.0 copy-start.3
  6.8 0.9 %copy-done.3 = bf16[128,1024]{1,0:T(8,128)(2,1)S(1)} copy-done((bf16[128,1024]{1,0:T(8,128)(2,1)S(1)}, bf16[128,1024]{1,0:T(8,128)(2,1)}, u32[]{:S(2)}) %copy-start.3) | copy-done | bytes 262168
  7.7 0.0 copy-start.4
  7.7 0.9 copy-done.4
  8.7 0.0 copy-start.5
  8.7 0.7 copy-done.5
  9.3 0.0 copy-start.6
  9.3 0.7 copy-done.6
  10.0 0.0 copy-start.7
  10.0 0.7 copy-done.7
  10.7 0.0 copy-start.8
  10.7 0.7 copy-done.8
  11.4 78.2 %swin.1 = bf16[64,1024]{1,0:T(8,128)(2,1)S(1)} custom-call(s32[2]{0:T(128)S(1)} %copy-done.8, bf16[4,64,512]{2,1,0:T(8,128)(2,1)S(1)} %bitcast.10, bf16[8,192,512]{2,1,0:T(8,128)(2,1)S(1)} %copy-done, bf16[512,512]{1,0:T(8,128)(2,1)S(1)} %copy-done.1, f32[1,512]{1,0:T(1,128)S(1)} %bitcast.15, s32[64,128]{1,0:T(8,128)S(1)} %get-tuple-element.5.rel0, ...), custom_call_target="tpu_custom_call" | custom-call | tf_op jit(solution)/shard_map/swin/pallas_call | solution.py:363
  89.6 0.7 copy.17
  (4 shorter events, 0.1 us)
Async XLA Ops:
  3.3 1.4 %copy-start = (bf16[8,192,512]{2,1,0:T(8,128)(2,1)S(1)}, bf16[8,192,512]{2,1,0:T(8,128)(2,1)}, u32[]{:S(2)}) copy-start(bf16[8,192,512]{2,1,0:T(8,128)(2,1)} %w0.1) | copy-start | bytes 4718596
  4.8 1.0 %copy-start.1 = (bf16[512,512]{1,0:T(8,128)(2,1)S(1)}, bf16[512,512]{1,0:T(8,128)(2,1)}, u32[]{:S(2)}) copy-start(bf16[512,512]{1,0:T(8,128)(2,1)} %wo0.1) | copy-start | bytes 1572868
  5.8 1.0 %copy-start.2 = (bf16[1,192,1024]{2,1,0:T(8,128)(2,1)S(1)}, bf16[1,192,1024]{2,1,0:T(8,128)(2,1)}, u32[]{:S(2)}) copy-start(bf16[1,192,1024]{2,1,0:T(8,128)(2,1)} %param.24) | copy-start | bytes 1179652
  6.8 0.9 %copy-start.3 = (bf16[128,1024]{1,0:T(8,128)(2,1)S(1)}, bf16[128,1024]{1,0:T(8,128)(2,1)}, u32[]{:S(2)}) copy-start(bf16[128,1024]{1,0:T(8,128)(2,1)} %wm.1) | copy-start | bytes 786436
  7.7 0.9 %copy-start.4 = (bf16[64,1024]{1,0:T(8,128)(2,1)S(1)}, bf16[64,1024]{1,0:T(8,128)(2,1)}, u32[]{:S(2)}) copy-start(bf16[64,1024]{1,0:T(8,128)(2,1)} %wo.1) | copy-start | bytes 393220
  8.7 0.7 copy-start.5
  9.3 0.7 copy-start.6
  10.0 0.7 copy-start.7
  10.7 0.7 copy-start.8

commit v2 on v1

v2 whole, which is shorter than its diff:
```python
import functools

import jax
import jax.numpy as jnp
from jax import lax
from jax.experimental import pallas as pl
from jax.experimental.pallas import tpu as pltpu
from jax.sharding import PartitionSpec as P

WIN = 8
EPS = 1e-05
NEG = -1e30
MESH = pl.DeviceIdType.MESH
F32 = jnp.float32
BF16 = jnp.bfloat16


def place():
    lat = lax.axis_index("lat")
    lon = lax.axis_index("lon")
    x = lax.div(lat, 4)
    half = lax.rem(lax.div(lat, 2), 2)
    core = lax.rem(lat, 2)
    y = half * 4 + lax.div(lon, 8)
    z = lax.rem(lon, 8)
    return lat, lon, x, y, z, core


def at(x, y, z, core):
    return (
        lax.rem(x + 4, 4) * 4 + lax.div(y, 4) * 2 + core,
        lax.rem(y, 4) * 8 + lax.rem(z + 8, 8),
    )


def dot_nt(left, right):
    return lax.dot_general(left, right, (((1,), (1,)), ((), ())), preferred_element_type=F32)


def dot_nn(left, right):
    return jnp.dot(left, right, preferred_element_type=F32)


def norm_rows(values, gain):
    mean = jnp.mean(values, axis=-1, keepdims=True)
    centred = values - mean
    spread = jnp.mean(centred * centred, axis=-1, keepdims=True)
    return centred * lax.rsqrt(spread + EPS) * gain


def lane_masks():
    lane = lax.broadcasted_iota(jnp.int32, (64, 128), 1)
    return lane < 64


def attend_pair(q2, k2, v2, bias, mask):
    low = lane_masks()
    low_b = low.astype(F32).astype(BF16)
    high_b = (1.0 - low.astype(F32)).astype(BF16)
    keys = jnp.concatenate([k2 * low_b, k2 * high_b], axis=0)
    scores = dot_nt(q2, keys) + bias
    if mask is not None:
        scores = scores + mask
    peak_a = jnp.max(jnp.where(low, scores, -jnp.inf), axis=-1, keepdims=True)
    peak_b = jnp.max(jnp.where(low, -jnp.inf, scores), axis=-1, keepdims=True)
    weights = jnp.exp(scores - jnp.where(low, peak_a, peak_b)).astype(BF16)
    values = jnp.concatenate([v2 * low_b, v2 * high_b], axis=0)
    ones = jnp.concatenate([low_b, high_b], axis=0)
    mixed = dot_nn(weights, jnp.concatenate([values, ones], axis=1))
    return (mixed[:, :128] / mixed[:, 128:]).astype(BF16)


def fill_bias(table, rel, rel2, out):
    coarse_part = table.astype(BF16).astype(F32)
    split = jnp.concatenate([coarse_part, table - coarse_part], axis=0).astype(BF16)
    entry = lax.broadcasted_iota(jnp.int32, (256, 256), 0)
    low = lax.broadcasted_iota(jnp.int32, (1, 128), 1) < 64
    rel2[...] = jnp.concatenate([rel[:32], rel[:32], rel[32:], rel[32:]], axis=1)

    def step(p, carry):
        row = rel2[pl.ds(p, 1), :]
        onehot = jnp.where(entry == row, 1.0, 0.0).astype(BF16)
        found = dot_nn(split, onehot)
        found = found[:8] + found[8:]
        for side in range(2):
            cols = slice(128 * side, 128 * side + 128)
            for t in range(4):
                out[t, pl.ds(p + 32 * side, 1), :] = jnp.where(
                    low, found[2 * t : 2 * t + 1, cols], found[2 * t + 1 : 2 * t + 2, cols]
                )
        return carry

    lax.fori_loop(0, 32, step, 0, unroll=4)


def kernel(
    shift, tok_h, w0_h, wo0_h, g0_h, rel0_h, bias0_h, gm_h, wm, g1_h, wq, wo, bias1_h, rel1_h,
    out,
    tok, w0, wo0, g0, rel0, bias0, gm, g1, bias1, rel1, tab0, rel2,
    fine_ref, hq, wide_m, wide_q, wide_o, tabs, b0, b1, mg, mo,
    part_s, part_r, upd_s, upd_r, coarse_ref, attn, ss, rs, ls,
):
    loads = [
        pltpu.make_async_copy(src, dst, ls.at[n])
        for n, (src, dst) in enumerate([
            (tok_h, tok), (bias1_h, bias1), (bias0_h, bias0), (rel0_h, rel0), (g0_h, g0),
            (w0_h, w0), (wo0_h, wo0), (gm_h, gm), (g1_h, g1), (rel1_h, rel1),
            (wm, wide_m.at[0]), (wq, wide_q.at[0]), (wo, wide_o.at[0]),
        ])
    ]
    for copy in loads:
        copy.start()
    lat, lon, x, y, z, core = place()
    half = lax.div(y, 4)
    a = shift[0]
    b = shift[1]

    to_xp, to_xm, to_x2 = at(x + 1, y, z, core), at(x - 1, y, z, core), at(x + 2, y, z, core)
    to_mir = at(x, 7 - y, z, core)
    to_yp, to_ym = at(x, lax.rem(y + 1, 8), z, core), at(x, lax.rem(y + 7, 8), z, core)
    to_zp, to_zm = at(x, y, z + 1, core), at(x, y, z - 1, core)
    to_core = at(x, y, z, 1 - core)
    to_pair = at(x, y + 1 - 2 * lax.rem(y, 2), z, core)
    depth = lax.rem(y, 4)
    edge = (depth == 0) | (depth == 3)
    outward = jnp.where(depth < 2, 7, 1)
    to_out = at(x, lax.rem(y + outward, 8), z, core)
    to_in = at(x, lax.rem(y + 8 - outward, 8), z, core)
    to_out2 = at(x, lax.rem(y + 2 * outward, 8), z, core)
    to_y2, to_ym2 = at(x, lax.rem(y + 2, 8), z, core), at(x, lax.rem(y + 6, 8), z, core)
    near, far = lax.rem(lat + 1 + 14 * core, 16), lax.rem(lat + 15 + 2 * core, 16)
    left, right = lax.rem(lon + 31, 32), lax.rem(lon + 1, 32)

    barrier = pltpu.get_barrier_semaphore()
    partners = [
        to_xp, to_xm, to_x2, to_mir, to_yp, to_ym, to_zp, to_zm, to_core,
        (far, lon), (lat, left), (lat, right), to_y2, to_ym2,
    ]
    for dev in partners:
        pl.semaphore_signal(barrier, inc=1, device_id=dev, device_id_type=MESH)
    loads[0].wait()
    for i in range(2):
        for j in range(2):
            block = tok[8 * i : 8 * i + 8].astype(F32)[:, 8 * j : 8 * j + 8, :]
            hq[4 * i + j + 5] = block.reshape(64, 512).astype(BF16)
    loads[1].wait()
    tabs[0] = jnp.zeros((8, 256), F32)
    tabs[0, :, 0:225] = jnp.broadcast_to(bias1[...], (8, 225))
    pl.semaphore_wait(barrier, len(partners))

    made = []

    def remote(src, dst, dev, take=None):
        k = len(made)
        copy = pltpu.make_async_remote_copy(
            src_ref=src, dst_ref=dst, send_sem=ss.at[k],
            recv_sem=rs.at[k if take is None else take],
            device_id=dev, device_id_type=MESH,
        )
        made.append(copy)
        return copy

    def start_all(copies):
        for copy in copies:
            copy.start()

    def recv_all(copies):
        for copy in copies:
            copy.wait_recv()

    far_at = 1 + 12 * core
    halo_near = [remote(hq.at[pl.ds(9 - 4 * core, 2)], hq.at[pl.ds(1 + 12 * core, 2)], (near, lon))]
    halo_far = [remote(hq.at[pl.ds(5 + 4 * core, 2)], hq.at[pl.ds(13 - 12 * core, 2)], (far, lon))]
    halo_lon = [
        remote(hq.at[6], hq.at[4], (lat, right)),
        remote(hq.at[10], hq.at[8], (lat, right)),
        remote(hq.at[5], hq.at[7], (lat, left)),
        remote(hq.at[9], hq.at[11], (lat, left)),
    ]
    corner_near = [
        remote(hq.at[8 - 4 * core], hq.at[12 * core], (near, lon)),
        remote(hq.at[11 - 4 * core], hq.at[3 + 12 * core], (near, lon)),
    ]
    corner_far = [
        remote(hq.at[far_at + 1], hq.at[far_at - 1], (lat, right)),
        remote(hq.at[far_at], hq.at[far_at + 2], (lat, left)),
    ]
    start_all(halo_lon + halo_near + halo_far)

    parity = lax.rem(z, 2)
    tab_first = [
        remote(tabs.at[0], tabs.at[2], to_xp),
        remote(tabs.at[0], tabs.at[1], to_xm),
        remote(tabs.at[0], tabs.at[3], to_x2),
        remote(tabs.at[0], tabs.at[4], to_mir),
    ]
    tab_second = [
        remote(tabs.at[4], tabs.at[6], to_xp),
        remote(tabs.at[4], tabs.at[5], to_xm),
        remote(tabs.at[4], tabs.at[7], to_x2),
    ]

    class Piece:
        def __init__(self, src, wide, base, rows, name):
            whole, by_y, direct = name in WHOLE, name in BY_Y, name in DIRECT
            size = rows // 2

            def parts(by):
                start = pl.multiple_of(base + by * size, 16)
                return (
                    pl.ds(start, size),
                    pl.ds(start, size // 2),
                    pl.ds(pl.multiple_of(start + size // 2, 16), size // 2),
                )

            part, part_a, part_b = parts(parity)
            side, side_a, side_b = parts(lax.rem(depth, 2) if by_y else parity)
            first = pl.ds(base, rows) if whole else side

            def swap(slot, count):
                slots = pl.ds(slot, count)
                return [
                    remote(wide.at[slots, part_a], wide.at[slots, part_a], to_zp),
                    remote(wide.at[slots, part_b], wide.at[slots, part_b], to_zm),
                ]

            def swap_y(slot, count):
                slots = pl.ds(slot, count)
                return [remote(wide.at[slots, side], wide.at[slots, side], to_pair)]

            self.whole = whole
            self.side = [
                remote(src.at[first], wide.at[2, first], to_xp),
                remote(src.at[first], wide.at[1, first], to_xm),
            ]
            take = len(made)
            self.cross = remote(src.at[part], wide.at[4, part], to_out)
            self.direct = direct
            if direct:
                self.inward = remote(src.at[part], wide.at[4, part], to_out2, take)
            else:
                self.inward = remote(wide.at[4, part], wide.at[4, part], to_in, take)
            self.on = [
                remote(wide.at[2, side_a], wide.at[3, side_a], to_xp),
                remote(wide.at[1, side_b], wide.at[3, side_b], to_xm),
            ]
            self.far_side = [
                remote(wide.at[4, part], wide.at[6, part], to_xp),
                remote(wide.at[4, part], wide.at[5, part], to_xm),
            ]
            self.far_on = [
                remote(wide.at[6, part_a], wide.at[7, part_a], to_xp),
                remote(wide.at[5, part_b], wide.at[7, part_b], to_xm),
            ]
            if by_y:
                self.swaps = [[] if whole else swap_y(1, 2), swap_y(3, 1), swap(4, 3), swap(7, 1)]
            else:
                self.swaps = [[] if whole else swap(1, 2), swap(3, 2), swap(5, 2), swap(7, 1)]

        def step(self, n):
            if n == 0:
                start_all(self.side)
                pl.when(edge)(self.cross.start)
                if self.direct:
                    pl.when(edge)(self.inward.start)
            if n == 1:
                recv_all(self.side)
                start_all(self.on)
                start_all(self.swaps[0])
            if n == 2:
                self.cross.wait_recv()
                if not self.direct:
                    pl.when(edge)(self.inward.start)
                start_all(self.far_side)
            if n == 3:
                recv_all(self.on)
                start_all(self.swaps[1])
            if n == 4:
                recv_all(self.far_side)
                start_all(self.far_on)
                start_all(self.swaps[2])
            if n == 5:
                recv_all(self.far_on)
                start_all(self.swaps[3])

        def finish(self, near):
            for swap in self.swaps[:2] if near else self.swaps[2:]:
                recv_all(swap)

        def sent(self):
            @pl.when(edge)
            def _():
                self.cross.wait_send()
                self.inward.wait_send()

    pieces = {
        "M": Piece(wm, wide_m, 0, 128, "M"),
        "A": Piece(wq, wide_q, 0, 128, "A"),
        "B": Piece(wq, wide_q, 128, 64, "B"),
        "W": Piece(wo, wide_o, 0, 64, "W"),
    }

    def events(name):
        for event in EVENTS[name]:
            if event == "T1":
                start_all(tab_first)
            elif event == "T2":
                recv_all(tab_first)
                start_all(tab_second)
            elif event == "CF":
                recv_all(halo_far)
                start_all(corner_far)
            else:
                pieces[event[1]].step(int(event[0]))

    events("B0")

    want = lax.broadcasted_iota(jnp.int32, (192, 1), 0)
    want_r = a + ((want & 63) >> 3)
    want_c = b + 8 * (want >> 6) + (want & 7)
    want = (want_r >> 3) * 256 + (want_c >> 3) * 64 + (want_r & 7) * 8 + (want_c & 7)
    pick = lax.broadcasted_iota(jnp.int32, (192, 512), 1) == want
    pick = jnp.where(pick, 1.0, 0.0).astype(BF16)
    for copy in loads[2:]:
        copy.wait()
    tab0[...] = jnp.zeros((8, 256), F32)
    tab0[:, 0:225] = bias0[...]
    fill_bias(tab0[...], rel0[...], rel2, b0)

    def window_row(k, carry):
        i = jnp.where(k == 0, 1, jnp.where(k == 1, 2 - 2 * core, 2 * core))

        @pl.when(k == 0)
        def _():
            events("R0a")
            recv_all(halo_lon)
            start_all(corner_near)

        @pl.when(k == 1)
        def _():
            events("R1a")
            recv_all(halo_near)
            recv_all(corner_near)

        @pl.when(k == 2)
        def _():
            events("R2a")
            recv_all(corner_far)

        cells = dot_nn(pick, hq[pl.ds(4 * i, 8)].reshape(512, 512))
        normed = norm_rows(cells, g0[...]).astype(BF16)
        query = (dot_nt(normed, w0[:, 0:64, :].reshape(512, 512)) * 0.125).astype(BF16)
        keys = dot_nt(normed, w0[:, 64:128, :].reshape(512, 512)).astype(BF16)
        values = dot_nt(normed, w0[:, 128:192, :].reshape(512, 512)).astype(BF16)
        for n in range(3):
            pl.when(k == n)(functools.partial(events, "R%db" % n))
        lane = lax.broadcasted_iota(jnp.int32, (1, 128), 1)
        row = lat * 16 + a - 8 + 8 * i + ((lane & 63) >> 3)
        mask = jnp.where((row >= 0) & (row < 256), 0.0, NEG)
        for w in range(3):
            rows = slice(64 * w, 64 * w + 64)
            for t in range(4):
                cols = slice(128 * t, 128 * t + 128)
                attn[rows, cols] = attend_pair(
                    query[rows, cols], keys[rows, cols], values[rows, cols], b0[t], mask
                )
        fine = cells + dot_nn(attn[...], wo0[...])
        fine_ref[pl.ds(pl.multiple_of(192 * i, 64), 192), :] = fine.astype(BF16)
        return carry

    lax.fori_loop(0, 3, window_row, 0)
    events("MG")

    want = lax.broadcasted_iota(jnp.int32, (256, 1), 0)
    want_r = 8 - a + 2 * ((want >> 3) & 7) + (want >> 7)
    want_c = 8 - b + 2 * (want & 7) + ((want >> 6) & 1)
    want = (want_r >> 3) * 192 + (want_c >> 3) * 64 + (want_r & 7) * 8 + (want_c & 7)
    pick = lax.broadcasted_iota(jnp.int32, (256, 576), 1) == want
    pick = jnp.where(pick, 1.0, 0.0).astype(BF16)
    picked = dot_nn(pick, fine_ref[...])
    blocks = [picked[64 * k : 64 * k + 64] for k in range(4)]
    total = sum(jnp.sum(block, axis=-1, keepdims=True) for block in blocks)
    mean = total * (1.0 / 2048)
    blocks = [block - mean for block in blocks]
    spread = sum(jnp.sum(block * block, axis=-1, keepdims=True) for block in blocks)
    scale = lax.rsqrt(spread * (1.0 / 2048) + EPS)
    for k in range(4):
        merged = (blocks[k] * scale * gm[:, 512 * k : 512 * k + 512]).astype(BF16)
        for m in range(4):
            chunk = 4 * k + m
            mg[chunk % 2, chunk // 2] = merged[:, 128 * m : 128 * m + 128]

    give_merged = remote(mg.at[1 - core], mo, to_core)
    give_part = remote(part_s, part_r, to_core)
    give_upd = remote(upd_s, upd_r, to_core)
    give_merged.start()
    events("B1")
    recv_all(tab_second)
    sub = lax.broadcasted_iota(jnp.int32, (8, 256), 0)
    table = jnp.zeros((8, 256), F32)
    for n, slot in enumerate(range(8)):
        table = jnp.where(sub == n, tabs[slot], table)
    fill_bias(table, rel1[...], rel2, b1)

    give_merged.wait_recv()
    slots = [
        2 * lax.rem(x + step, 4) + side for side in (half, 1 - half) for step in (0, 1, 3, 2)
    ]
    mine = jnp.concatenate([mg[core, slot] for slot in slots], axis=1)
    theirs = jnp.concatenate([mo[slot] for slot in slots], axis=1)
    merged = jnp.concatenate([theirs, mine], axis=0)
    events("MM")
    pieces["M"].finish(True)
    partial = dot_nn(merged[:, :512], wide_m[0:4].reshape(512, 1024))
    events("MF")
    pieces["M"].finish(False)
    partial = partial + dot_nn(merged[:, 512:], wide_m[4:8].reshape(512, 1024))
    part_s[...] = partial.astype(BF16)
    give_part.start()
    events("LN")
    give_part.wait_recv()
    coarse = (partial[64:] + part_r[0:64].astype(F32)).astype(BF16)
    coarse_ref[...] = coarse
    others = (partial[:64] + part_r[64:128].astype(F32)).astype(BF16)
    both = jnp.concatenate([coarse, others], axis=0).astype(F32)
    normed = norm_rows(both, g1[...]).astype(BF16)
    for g in range(2):
        events("QN" if g == 0 else "QF")
        pieces["A"].finish(g == 0)
        pieces["B"].finish(g == 0)
        heads = slice(4 * g, 4 * g + 4)
        query = dot_nt(normed, wide_q[heads, 0:64, :].reshape(256, 1024)) * 0.125
        query = query.astype(BF16)
        keys = dot_nt(normed, wide_q[heads, 64:128, :].reshape(256, 1024)).astype(BF16)
        values = dot_nt(normed, wide_q[heads, 128:192, :].reshape(256, 1024)).astype(BF16)
        for w in range(2):
            rows = slice(64 * w, 64 * w + 64)
            for t in range(2):
                cols = slice(128 * t, 128 * t + 128)
                pair = 2 * g + t
                attn[rows, 128 * pair : 128 * pair + 128] = attend_pair(
                    query[rows, cols], keys[rows, cols], values[rows, cols], b1[pair], None
                )
    events("WO")
    pieces["W"].finish(True)
    pieces["W"].finish(False)
    update = dot_nn(attn[0:128, :], wide_o[...].reshape(512, 1024))
    upd_s[...] = update[64:].astype(BF16)
    give_upd.start()
    give_upd.wait_recv()
    out[...] = (coarse_ref[...].astype(F32) + update[:64] + upd_r[...].astype(F32)).astype(BF16)
    for piece in pieces.values():
        piece.sent()
    conditional = [c for piece in pieces.values() for c in (piece.cross, piece.inward)]
    for copy in made:
        if not any(copy is c for c in conditional):
            copy.wait_send()


COPIES = 10 + 7 + 4 * 18 + 3
WHOLE = ""
BY_Y = "BW"
DIRECT = "ABMW"
EVENTS = {
    "B0": ("T1", "0M",),
    "R0a": ("0A",),
    "R0b": ("1A", "1M",),
    "R1a": ("0B", "0W",),
    "R1b": ("CF", "2M", "3M",),
    "R2a": ("1B", "4M",),
    "R2b": ("2A", "3B", "3A",),
    "MG": ("2B", "5M", "T2",),
    "B1": ("4A", "2W", "4B", "1W",),
    "MM": ("5A",),
    "MF": (),
    "LN": ("5B", "4W",),
    "QN": ("3W", "5W",),
    "QF": (),
    "WO": (),
}


def on_device(
    tokens, w_qkv0, w_out0, gain0, bias0, rel0, shift, gain_merge, w_merge, gain1, w_qkv1,
    w_out1, bias1, rel1,
):
    vmem = pl.BlockSpec(memory_space=pltpu.VMEM)
    hbm = pl.BlockSpec(memory_space=pltpu.HBM)
    smem = pl.BlockSpec(memory_space=pltpu.SMEM)
    result = pl.pallas_call(
        kernel,
        out_shape=jax.ShapeDtypeStruct((64, 1024), BF16),
        in_specs=[smem] + [hbm] * 13,
        out_specs=vmem,
        scratch_shapes=[
            pltpu.VMEM((16, 16, 512), BF16),
            pltpu.VMEM((8, 192, 512), BF16),
            pltpu.VMEM((512, 512), BF16),
            pltpu.VMEM((1, 512), F32),
            pltpu.VMEM((64, 64), jnp.int32),
            pltpu.VMEM((8, 225), F32),
            pltpu.VMEM((1, 2048), F32),
            pltpu.VMEM((1, 1024), F32),
            pltpu.VMEM((1, 225), F32),
            pltpu.VMEM((64, 64), jnp.int32),
            pltpu.VMEM((8, 256), F32),
            pltpu.VMEM((32, 256), jnp.int32),
            pltpu.VMEM((576, 512), BF16),
            pltpu.VMEM((16, 64, 512), BF16),
            pltpu.VMEM((8, 128, 1024), BF16),
            pltpu.VMEM((8, 192, 1024), BF16),
            pltpu.VMEM((8, 64, 1024), BF16),
            pltpu.VMEM((8, 8, 256), F32),
            pltpu.VMEM((4, 64, 128), F32),
            pltpu.VMEM((4, 64, 128), F32),
            pltpu.VMEM((2, 8, 64, 128), BF16),
            pltpu.VMEM((8, 64, 128), BF16),
            pltpu.VMEM((128, 1024), BF16),
            pltpu.VMEM((128, 1024), BF16),
            pltpu.VMEM((64, 1024), BF16),
            pltpu.VMEM((64, 1024), BF16),
            pltpu.VMEM((64, 1024), BF16),
            pltpu.VMEM((192, 512), BF16),
            pltpu.SemaphoreType.DMA((COPIES,)),
            pltpu.SemaphoreType.DMA((COPIES,)),
            pltpu.SemaphoreType.DMA((13,)),
        ],
        compiler_params=pltpu.CompilerParams(
            collective_id=0, has_side_effects=True, vmem_limit_bytes=60 << 20
        ),
        name="swin",
    )(
        shift, tokens, w_qkv0, w_out0, gain0.reshape(1, 512), rel0, bias0,
        gain_merge.reshape(1, 2048), w_merge, gain1.reshape(1, 1024),
        w_qkv1.reshape(192, 1024), w_out1, bias1, rel1,
    )
    return result.reshape(8, 8, 1024)


def solution(mesh):
    placed = (
        P("lat", "lon", None),
        P(),
        P(),
        P(),
        P(),
        P(),
        P(),
        P(),
        P("lat", None),
        P(),
        P("lat", None, None),
        P("lat", None),
        P("lat", None),
        P(),
    )
    return jax.shard_map(
        on_device, mesh=mesh, in_specs=placed, out_specs=P("lat", "lon", None), check_vma=False
    )
```

time: 90.8 us -> 64 us (0.70)
  the two profiles are of different devices: /device:TPU:57 before, /device:TPU:1 now
where the time goes in v2:
time: 64 us; the launch traced here: 63.8 us
  Pallas kernels  62.3 us (97%)
  local copies, waits for them, and re-layouts  1.57 us (2%)
    pallas_call x1, Pallas kernels, on_device(): pl.pallas_call(kernel, out_shape=jax.ShapeDtypeStruct((64, 1024), BF16),...  62.3 us
    unnamed x1, local copies, waits for them, and re-layouts  1.57 us

profile of v2, /device:TPU:1, one launch (start us, length us, event | category | flops | bytes accessed | tf_op | source)
XLA Modules:
  0.0 63.8 jit_solution(15624931587772645926)
XLA Ops:
  0.0 62.3 %swin.1 = bf16[64,1024]{1,0:T(8,128)(2,1)} custom-call(s32[2]{0:T(128)} %shift.1, bf16[16,16,512]{2,1,0:T(8,128)(2,1)} %tok_h.1, bf16[8,192,512]{2,1,0:T(8,128)(2,1)} %w0_h.1, bf16[512,512]{1,0:T(8,128)(2,1)} %wo0_h.1, f32[1,512]{1,0:T(1,128)} %bitcast.9, s32[64,64]{1,0:T(8,128)} %rel0_h.1, f32[8,225]{1,0:T(8,128)} %bias0_h.1, f32[1,2048]{1,0:T(1,128)} %bitcast.7, ...), custom_call_target="tpu_custom_call" | custom-call | tf_op jit(solution)/shard_map/swin/pallas_call | solution.py:490
  62.3 1.6 %copy.16 = bf16[8,8,1024]{2,1,0:T(8,128)(2,1)} copy(bf16[8,8,1024]{2,1,0:T(8,128)(2,1)} %bitcast.5) | data formatting | bytes 262144

commit v3 on v2

--- a/solution.py
+++ b/solution.py
@@ -444,11 +444,12 @@
     events("WO")
     pieces["W"].finish(True)
     pieces["W"].finish(False)
-    update = dot_nn(attn[0:128, :], wide_o[...].reshape(512, 1024))
-    upd_s[...] = update[64:].astype(BF16)
+    w_out = wide_o[...].reshape(512, 1024)
+    upd_s[...] = dot_nn(attn[64:128, :], w_out).astype(BF16)
     give_upd.start()
+    update = coarse_ref[...].astype(F32) + dot_nn(attn[0:64, :], w_out)
     give_upd.wait_recv()
-    out[...] = (coarse_ref[...].astype(F32) + update[:64] + upd_r[...].astype(F32)).astype(BF16)
+    out[...] = (update + upd_r[...].astype(F32)).astype(BF16).reshape(8, 8, 1024)
     for piece in pieces.values():
         piece.sent()
     conditional = [c for piece in pieces.values() for c in (piece.cross, piece.inward)]
@@ -458,23 +459,23 @@
 
 
 COPIES = 10 + 7 + 4 * 18 + 3
-WHOLE = ""
-BY_Y = "BW"
+WHOLE = "BW"
+BY_Y = "ABW"
 DIRECT = "ABMW"
 EVENTS = {
-    "B0": ("T1", "0M",),
-    "R0a": ("0A",),
-    "R0b": ("1A", "1M",),
-    "R1a": ("0B", "0W",),
-    "R1b": ("CF", "2M", "3M",),
-    "R2a": ("1B", "4M",),
-    "R2b": ("2A", "3B", "3A",),
-    "MG": ("2B", "5M", "T2",),
-    "B1": ("4A", "2W", "4B", "1W",),
-    "MM": ("5A",),
-    "MF": (),
-    "LN": ("5B", "4W",),
-    "QN": ("3W", "5W",),
+    "B0": ("T1", "0M", "0B",),
+    "R0a": ("1M", "0A", "1B", "0W",),
+    "R0b": (),
+    "R1a": ("2M", "CF", "3M",),
+    "R1b": ("2B", "1A", "3B",),
+    "R2a": ("4M", "4B", "1W",),
+    "R2b": ("3A", "2A",),
+    "MG": ("5M", "5B", "2W", "T2",),
+    "B1": ("4A",),
+    "MM": (),
+    "MF": ("3W",),
+    "LN": ("5A", "4W",),
+    "QN": ("5W",),
     "QF": (),
     "WO": (),
 }
@@ -489,7 +490,7 @@
     smem = pl.BlockSpec(memory_space=pltpu.SMEM)
     result = pl.pallas_call(
         kernel,
-        out_shape=jax.ShapeDtypeStruct((64, 1024), BF16),
+        out_shape=jax.ShapeDtypeStruct((8, 8, 1024), BF16),
         in_specs=[smem] + [hbm] * 13,
         out_specs=vmem,
         scratch_shapes=[
@@ -534,7 +535,7 @@
         gain_merge.reshape(1, 2048), w_merge, gain1.reshape(1, 1024),
         w_qkv1.reshape(192, 1024), w_out1, bias1, rel1,
     )
-    return result.reshape(8, 8, 1024)
+    return result
 
 
 def solution(mesh):

time: 64 us -> 63.3 us (0.989)
  Pallas kernels: 62.3 us -> 61.6 us
    pallas_call x1, Pallas kernels: 62.3 us -> 61.6 us  [on_device(): pl.pallas_call(kernel, out_shape=jax.ShapeDtypeStruct((8, 8, 1024), BF16)...]
where the time goes in v3:
time: 63.3 us; the launch traced here: 63.2 us
  Pallas kernels  61.6 us (97%)
  local copies, waits for them, and re-layouts  1.57 us (2%)
    pallas_call x1, Pallas kernels, on_device(): pl.pallas_call(kernel, out_shape=jax.ShapeDtypeStruct((8, 8, 1024), BF16)...  61.6 us
    unnamed x1, local copies, waits for them, and re-layouts  1.57 us

profile of v3, /device:TPU:1, one launch (start us, length us, event | category | flops | bytes accessed | tf_op | source)
XLA Modules:
  0.0 63.2 jit_solution(3318919973899770509)
XLA Ops:
  0.0 61.6 %swin.1 = bf16[8,8,1024]{2,1,0:T(8,128)(2,1)} custom-call(s32[2]{0:T(128)} %shift.1, bf16[16,16,512]{2,1,0:T(8,128)(2,1)} %tok_h.1, bf16[8,192,512]{2,1,0:T(8,128)(2,1)} %w0_h.1, bf16[512,512]{1,0:T(8,128)(2,1)} %wo0_h.1, f32[1,512]{1,0:T(1,128)} %bitcast.7, s32[64,64]{1,0:T(8,128)} %rel0_h.1, f32[8,225]{1,0:T(8,128)} %bias0_h.1, f32[1,2048]{1,0:T(1,128)} %bitcast.5, ...), custom_call_target="tpu_custom_call" | custom-call | tf_op jit(solution)/shard_map/swin/pallas_call | solution.py:491
  61.6 1.6 %copy.16 = bf16[8,8,1024]{2,1,0:T(8,128)(2,1)} copy(bf16[8,8,1024]{2,1,0:T(8,128)(2,1)} %swin.1) | data formatting | bytes 262144

commit v4 on v3

--- a/solution.py
+++ b/solution.py
@@ -459,7 +459,7 @@
 
 
 COPIES = 10 + 7 + 4 * 18 + 3
-WHOLE = "BW"
+WHOLE = ""
 BY_Y = "ABW"
 DIRECT = "ABMW"
 EVENTS = {

time: 63.3 us -> 62.1 us (0.981)
  Pallas kernels: 61.6 us -> 60.4 us
    pallas_call x1, Pallas kernels: 61.6 us -> 60.4 us  [on_device(): pl.pallas_call(kernel, out_shape=jax.ShapeDtypeStruct((8, 8, 1024), BF16)...]
where the time goes in v4:
time: 62.1 us; the launch traced here: 62 us
  Pallas kernels  60.4 us (97%)
  local copies, waits for them, and re-layouts  1.57 us (3%)
    pallas_call x1, Pallas kernels, on_device(): pl.pallas_call(kernel, out_shape=jax.ShapeDtypeStruct((8, 8, 1024), BF16)...  60.4 us
    unnamed x1, local copies, waits for them, and re-layouts  1.57 us

profile of v4, /device:TPU:1, one launch (start us, length us, event | category | flops | bytes accessed | tf_op | source)
XLA Modules:
  0.0 62.0 jit_solution(2919297965001350489)
XLA Ops:
  0.0 60.4 %swin.1 = bf16[8,8,1024]{2,1,0:T(8,128)(2,1)} custom-call(s32[2]{0:T(128)} %shift.1, bf16[16,16,512]{2,1,0:T(8,128)(2,1)} %tok_h.1, bf16[8,192,512]{2,1,0:T(8,128)(2,1)} %w0_h.1, bf16[512,512]{1,0:T(8,128)(2,1)} %wo0_h.1, f32[1,512]{1,0:T(1,128)} %bitcast.7, s32[64,64]{1,0:T(8,128)} %rel0_h.1, f32[8,225]{1,0:T(8,128)} %bias0_h.1, f32[1,2048]{1,0:T(1,128)} %bitcast.5, ...), custom_call_target="tpu_custom_call" | custom-call | tf_op jit(solution)/shard_map/swin/pallas_call | solution.py:491
  60.4 1.6 %copy.16 = bf16[8,8,1024]{2,1,0:T(8,128)(2,1)} copy(bf16[8,8,1024]{2,1,0:T(8,128)(2,1)} %swin.1) | data formatting | bytes 262144
